TPU v7x, 256 devices: a whole 4x4x8 slice. The times are simulated.
256 devices in a mesh: sec: 64 (over z, x, core), mpo: 4 (over y).
Axes of the slice: x: 4, y: 4, z: 8, core: 2. Of those that a mesh axis runs over, the one named last changes fastest.
Arguments:
- wavefunction: bfloat16 [2048, 128, 128], P('sec'), may hold values from -100 to 100
- energy_shift: float32 [1], replicated, may hold values from 0.5 to 2
- left_env: bfloat16 [20, 2048, 128, 128], P('mpo', 'sec'), may hold values from -0.125 to 0.125
- right_env: bfloat16 [20, 2048, 128, 128], P('mpo', 'sec'), may hold values from -0.5 to 0.5
- target: int32 [20, 2048], P('mpo', 'sec'), may hold values from 0 to 2047, as said below
Outputs:
- second_image: bfloat16 [2048, 128, 128], P('sec')
Inputs may be any that keep to these rules, and one draw needn't show every extreme that they name: `target`: for any device's blocks along sec and MPO terms of one device along mpo (terms j * 5 to (j + 1) * 5 - 1), at most 3 couplings point into the 32 blocks of one device, and that many do for some pair in every draw.
All inputs are finite; a program needn't handle non-finite values.
Results may differ from a plain program's by a relative error of at most 0.007.
Values may be sent and summed in bfloat16 or wider, within the bound.
A program may use at most 128 MiB of HBM per device.

v0:
```python
import jax
import jax.numpy as jnp
from jax import lax
from jax.sharding import PartitionSpec as P

epsilon = 1e-06


def route_tables(target, sec_count):
    terms_here, blocks_here = target.shape
    item_count = terms_here * blocks_here
    capacity = (item_count + sec_count - 1) // sec_count
    targets = target.reshape(item_count)
    owner_dev = targets // blocks_here
    ordinal = jnp.arange(item_count, dtype=jnp.int32)
    same_owner = owner_dev[:, None] == owner_dev[None, :]
    earlier = ordinal[None, :] < ordinal[:, None]
    slot_rank = jnp.sum((same_owner & earlier).astype(jnp.int32), axis=1)
    slot_index = owner_dev * capacity + slot_rank
    slot_item = jnp.full((sec_count * capacity,), item_count, jnp.int32).at[slot_index].set(ordinal)
    tag_value = ordinal // blocks_here * blocks_here + targets % blocks_here
    slot_tag = jnp.full((sec_count * capacity,), -1, jnp.int32).at[slot_index].set(tag_value)
    return (slot_item, slot_tag)


def partial_image(vector, left_env, right_env, slot_item, slot_tag):
    terms_here, blocks_here, row_size, col_size = right_env.shape
    item_count = terms_here * blocks_here
    products = jnp.einsum("sij,wsjk->wsik", vector, right_env, preferred_element_type=jnp.float32)
    products = products.astype(jnp.bfloat16).reshape(item_count, row_size, col_size)
    padded = jnp.concatenate([products, jnp.zeros((1, row_size, col_size), jnp.bfloat16)], axis=0)
    outgoing = jnp.take(padded, slot_item, axis=0)
    arrived, tags_in = (
        lax.all_to_all(outgoing, "sec", split_axis=0, concat_axis=0, tiled=True),
        lax.all_to_all(slot_tag, "sec", split_axis=0, concat_axis=0, tiled=True),
    )
    selector = (tags_in[None, :] == jnp.arange(item_count, dtype=jnp.int32)[:, None]).astype(
        jnp.bfloat16
    )
    summed = jnp.dot(
        selector,
        arrived.reshape(arrived.shape[0], row_size * col_size),
        preferred_element_type=jnp.float32,
    )
    summed = summed.astype(jnp.bfloat16).reshape(terms_here, blocks_here, row_size, col_size)
    return jnp.einsum("wtij,wtjk->tik", left_env, summed, preferred_element_type=jnp.float32)


def combine_whole(partial_terms):
    return lax.psum(partial_terms, "mpo")


def body(wavefunction, energy_shift, left_env, right_env, target):
    sec_count = lax.axis_size("sec")
    blocks_here, row_size, col_size = wavefunction.shape
    total_cells = sec_count * blocks_here * row_size * col_size
    slot_item, slot_tag = route_tables(target, sec_count)
    first_terms = partial_image(wavefunction, left_env, right_env, slot_item, slot_tag)
    image_sum = combine_whole(first_terms)
    correction = image_sum - energy_shift[0] * wavefunction.astype(jnp.float32)
    corr_squares = lax.psum(jnp.sum(correction * correction), "sec")
    second_vector = (correction / jnp.sqrt(corr_squares / total_cells + epsilon)).astype(
        jnp.bfloat16
    )
    second_terms = partial_image(second_vector, left_env, right_env, slot_item, slot_tag)
    result = combine_whole(second_terms).astype(jnp.bfloat16)
    return result


def solution(mesh):
    placed = (
        P("sec", None, None),
        P(),
        P("mpo", "sec", None, None),
        P("mpo", "sec", None, None),
        P("mpo", "sec"),
    )
    return jax.shard_map(
        body, mesh=mesh, in_specs=placed, out_specs=P("sec", None, None), check_vma=False
    )
```

profile of v0, /device:TPU:4, one launch (start us, length us, event | category | flops | bytes accessed | tf_op | source)
XLA Modules:
  0.0 646.8 jit_solution(8769576261925471160)
XLA Ops:
  6.5 0.8 reshape.159
  7.3 0.8 reshape.158
  8.1 0.2 convert_reduce_fusion
  8.3 1.1 scatter_custom_fusion
  9.4 0.8 all_to_all.13
  10.1 12.0 %all-to-all-start = ((s32[64,3,1]{1,2,0:T(1,128)}), s32[64,3,1]{1,2,0:T(1,128)S(1)}, u32[]{:S(2)}, u32[]{:S(2)}) async-start(s32[64,3,1]{1,2,0:T(1,128)} %bitcast.2), calls=%async_computation | async-start | bytes 65536 | tf_op jit(solution)/shard_map/all_to_all | solution.py:35
  22.1 1.1 scatter_custom_fusion.1
  23.3 6.7 %convert_bitcast_fusion.1 = bf16[5,32,128,128]{2,3,0,1:T(8,128)(2,1)} fusion(bf16[5,32,128,128]{3,2,1,0:T(8,128)(2,1)} %param.10, bf16[32,128,128]{2,1,0:T(8,128)(2,1)} %param.7), kind=kOutput, calls=%fused_computation.17 | convolution fusion | flops 673710080 | bytes 11534336 | tf_op jit(solution)/shard_map/sij,wsjk->wsik/dot_general | solution.py:29
  30.0 7.8 %copy.38 = bf16[5,32,128,128]{3,2,1,0:T(8,128)(2,1)} copy(bf16[5,32,128,128]{2,3,0,1:T(8,128)(2,1)} %convert_bitcast_fusion.1) | data formatting | bytes 10485760 | tf_op jit(solution)/shard_map/convert_element_type | solution.py:30
  37.8 6.9 %concatenate.6 = bf16[161,128,128]{2,1,0:T(8,128)(2,1)} pad(bf16[160,128,128]{2,1,0:T(8,128)(2,1)} %bitcast.71, bf16[]{:T(256)} %constant.61.clone.1), padding=0_1x0_0x0_0 | pad | bytes 10518530 | tf_op jit(solution)/shard_map/concatenate | solution.py:31
  44.7 10.5 %gather_fusion = bf16[192,128,128]{2,1,0:T(8,128)(2,1)} fusion(bf16[161,128,128]{2,1,0:T(8,128)(2,1)} %concatenate.6, s32[1024]{0:T(1024)S(1)} %pad_clamp_fusion), kind=kCustom, calls=%fused_computation.clone | custom fusion | bytes 12583680 | tf_op jit(solution)/shard_map/jit(_take)/gather | solution.py:32
  55.2 6.1 broadcast_select_fusion
  61.3 0.0 all-to-all-done
  61.3 0.0 slice-start
  61.3 10.6 %all-to-all-start.1 = ((bf16[192,128,128]{2,1,0:T(8,128)(2,1)}), bf16[192,128,128]{2,1,0:T(8,128)(2,1)}, u32[]{:S(2)}, u32[]{:S(2)}) async-start(bf16[192,128,128]{2,1,0:T(8,128)(2,1)} %broadcast_select_fusion), calls=%async_computation.1 | async-start | bytes 12582912 | tf_op jit(solution)/shard_map/all_to_all | solution.py:34
  71.9 0.2 all-reduce.5.cloned.1.call-start
  72.1 0.5 broadcast.175
  72.6 0.7 reduce.3
  73.4 0.1 eq.19
  73.5 139.6 %all-to-all-done.1 = bf16[192,128,128]{2,1,0:T(8,128)(2,1)} async-done(((bf16[192,128,128]{2,1,0:T(8,128)(2,1)}), bf16[192,128,128]{2,1,0:T(8,128)(2,1)}, u32[]{:S(2)}, u32[]{:S(2)}) %all-to-all-start.1) | async-done | bytes 6291488 | tf_op jit(solution)/shard_map/all_to_all | solution.py:34
  213.1 0.0 slice-start.1
  213.1 7.4 %fusion.16 = bf16[20,8,128,128]{3,1,2,0:T(8,128)(2,1)S(1)} fusion(bf16[24,8,128,128]{3,2,1,0:T(8,128)(2,1)} %bitcast.20, s32[192]{0:T(256)S(1)} %eq.19), kind=kOutput, calls=%fused_computation.22 | convolution fusion | flops 1009285120 | bytes 11535104 | tf_op jit(solution)/shard_map/dot_general | solution.py:40
  220.5 1.5 copy.55
  222.0 0.0 slice-done
  222.0 0.0 slice-done.1
  222.1 0.0 copy-start
  222.1 3.3 fusion.22
  225.3 0.0 all-reduce.5.cloned.1.call-update
  225.4 0.0 copy-done
  225.4 0.7 copy.40
  226.7 59.3 %all-reduce.5.cloned.1.call-done = f32[32,128,128]{1,2,0:T(8,128)} async-done(((f32[32,128,128]{1,2,0:T(8,128)}), f32[32,128,128]{1,2,0:T(8,128)}) %all-reduce.5.cloned.1.call-update) | async-done | bytes 2097168 | tf_op jit(solution)/shard_map/psum | solution.py:50
  286.0 2.7 multiply_reduce_fusion
  288.7 119.6 %psum.22 = f32[]{:T(128)} all-reduce(f32[]{:T(128)} %multiply_reduce_fusion), channel_id=1, replica_groups=mesh['sec'=64,'mpo'=4] {'sec'}, use_global_device_ids=true, to_apply=%region_5.7 | all-reduce | flops 1 | bytes 8 | tf_op jit(solution)/shard_map/psum | solution.py:61
  409.0 4.7 convert_bitcast_fusion
  413.7 2.1 copy.43
  415.8 3.5 concatenate.7
  419.3 10.5 %gather_fusion.1 = bf16[192,128,128]{2,1,0:T(8,128)(2,1)} fusion(bf16[161,128,128]{2,1,0:T(8,128)(2,1)} %concatenate.7, s32[1024]{0:T(1024)S(1)} %pad_clamp_fusion), kind=kCustom, calls=%fused_computation.1.clone | custom fusion | bytes 12583680 | tf_op jit(solution)/shard_map/jit(_take)/gather | solution.py:32
  429.8 3.4 broadcast_select_fusion.1
  433.3 0.0 slice-start.2
  433.3 156.4 %all_to_all.20 = bf16[192,128,128]{2,1,0:T(8,128)(2,1)S(1)} all-to-all(bf16[192,128,128]{2,1,0:T(8,128)(2,1)S(1)} %broadcast_select_fusion.1), channel_id=1, replica_groups=mesh['sec'=64,'mpo'=4] {'sec'}, dimensions={0} | all-to-all | bytes 12582912 | tf_op jit(solution)/shard_map/all_to_all | solution.py:34
  589.7 0.0 slice-start.3
  589.7 4.5 fusion.19
  594.2 1.5 copy.57
  595.7 0.0 slice-done.2
  595.7 0.0 slice-done.3
  595.8 2.0 fusion.25
  597.8 40.9 %all-reduce.6 = bf16[32,128,128]{1,2,0:T(8,128)(2,1)S(1)} all-reduce(f32[32,128,128]{1,2,0:T(8,128)S(1)} %fusion.25), channel_id=1, replica_groups=mesh['sec'=64,'mpo'=4] {'mpo'}, use_global_device_ids=true, to_apply=%region_6.8 | all-reduce | flops 524288 | bytes 3145728 | tf_op jit(solution)/shard_map/psum | solution.py:50
  638.6 1.3 copy.45
  (8 shorter events, 0.0 us)
Async XLA Ops:
  10.1 51.2 %all-to-all-start = ((s32[64,3,1]{1,2,0:T(1,128)}), s32[64,3,1]{1,2,0:T(1,128)S(1)}, u32[]{:S(2)}, u32[]{:S(2)}) async-start(s32[64,3,1]{1,2,0:T(1,128)} %bitcast.2), calls=%async_computation | async-start | bytes 65536 | tf_op jit(solution)/shard_map/all_to_all | solution.py:35
  61.3 160.7 %slice-start = ((s8[5242880]{0:T(1024)(128)(4,1)}), s8[1048576]{0:T(1024)(128)(4,1)S(1)}, s32[]{:S(2)}) async-start(s8[5242880]{0:T(1024)(128)(4,1)} %bitcast.66), calls=%async_computation.4 | async-start | bytes 2097152
  61.3 151.8 %all-to-all-start.1 = ((bf16[192,128,128]{2,1,0:T(8,128)(2,1)}), bf16[192,128,128]{2,1,0:T(8,128)(2,1)}, u32[]{:S(2)}, u32[]{:S(2)}) async-start(bf16[192,128,128]{2,1,0:T(8,128)(2,1)} %broadcast_select_fusion), calls=%async_computation.1 | async-start | bytes 12582912 | tf_op jit(solution)/shard_map/all_to_all | solution.py:34
  71.9 214.1 %all-reduce.5.cloned.1.call-start = ((), (), s32[]{:S(2)}) async-start(), calls=%async_computation.3 | async-start | bytes 4194304 | tf_op jit(solution)/shard_map/psum | solution.py:50
  213.1 9.0 %slice-start.1 = ((s8[5242880]{0:T(1024)(128)(4,1)}), s8[4194304]{0:T(1024)(128)(4,1)S(1)}, s32[]{:S(2)}) async-start(s8[5242880]{0:T(1024)(128)(4,1)} %bitcast.66), calls=%async_computation.5 | async-start | bytes 8388608
  222.1 3.3 copy-start
  433.3 162.5 %slice-start.2 = ((s8[5242880]{0:T(1024)(128)(4,1)}), s8[1048576]{0:T(1024)(128)(4,1)S(1)}, s32[]{:S(2)}) async-start(s8[5242880]{0:T(1024)(128)(4,1)} %bitcast.68), calls=%async_computation.6 | async-start | bytes 2097152
  589.7 6.1 slice-start.3
Sparse Core Ops, SparseCore 0:
  225.5 60.4 all-reduce.4
where the time goes:
time: 648 us; the launch traced here: 647 us
  blocking collectives  317 us (49%)
  waiting for transfers between devices  199 us (31%)
  local copies, waits for them, and re-layouts  51.6 us (8%)
  matrix products  28.5 us (4%)
  starting transfers between devices  22.8 us (4%)
  between operations  14.9 us (2%)
  other arithmetic  13.2 us (2%)
    all_to_all x1, blocking collectives, partial_image(): lax.all_to_all(outgoing, 'sec', split_axis=0, concat_axis=0, tiled=True)  156 us
    all_to_all x1, waiting for transfers between devices, partial_image(): lax.all_to_all(outgoing, 'sec', split_axis=0, concat_axis=0, tiled=True)  140 us
    psum x1, blocking collectives, body(): corr_squares = lax.psum(jnp.sum(correction * correction), 'sec')  120 us
    psum x1, waiting for transfers between devices, combine_whole(): return lax.psum(partial_terms, 'mpo')  59.3 us
    psum x1, blocking collectives, combine_whole(): return lax.psum(partial_terms, 'mpo')  40.9 us
    gather x2, local copies, waits for them, and re-layouts, partial_image(): outgoing = jnp.take(padded, slot_item, axis=0)  21.1 us
  transfers between devices with their start and end apart: 3, of which 2 were waited for; matrix products, arithmetic and copies ran while one was open for 6% of the time, Pallas kernels for 0%

commit v1 on v0

v1 whole, which is shorter than its diff:
```python
import functools

import jax
import jax.numpy as jnp
from jax import lax
from jax.experimental import pallas as pl
from jax.experimental.pallas import tpu as pltpu
from jax.sharding import PartitionSpec as P

MESH = pl.DeviceIdType.MESH
EPSILON = 1e-06
NZ, NX, NC, NY = 8, 4, 2, 4
PEERS = NZ * NX * NC
CAP = 3
SLOTS = PEERS * CAP
B = 128
BLOCKS = 32
TERMS = 5
ITEMS = TERMS * BLOCKS
CHUNKS = 4
ROWS = B // CHUNKS
QUARTER = BLOCKS // NY
NT = (((1,), (1,)), ((), ()))
NN = (((1,), (0,)), ((), ()))


def coordinates():
    sec = lax.axis_index("sec")
    return sec // (NX * NC), (sec // NC) % NX, sec % NC, lax.axis_index("mpo")


def peer_of(offset, here):
    z, x, core, y = here
    dz, dx, dc = offset // (NX * NC), (offset // NC) % NX, offset % NC
    return (((z + dz) % NZ * NX + (x + dx) % NX) * NC + (core + dc) % NC, y)


def offset_at(i):
    zi, rest = i % NZ, (PEERS // NZ - 1) - i // NZ
    dist, sign = NZ // 2 - (zi + 1) // 2, 2 * (zi % 2) - 1
    return (dist * sign + NZ) % NZ * (NX * NC) + rest


def slot_tables(target, here):
    z, x, core, _ = here
    f32 = jnp.float32
    wide = jnp.concatenate([target, jnp.zeros((TERMS, B - BLOCKS), jnp.int32)], axis=1)
    padded = jnp.concatenate([wide, jnp.zeros((8 - TERMS, B), jnp.int32)], axis=0)
    device, local = padded >> 5, padded & (BLOCKS - 1)
    dz = ((device >> 3) - z + NZ) & (NZ - 1)
    dx = (((device >> 1) & (NX - 1)) - x + NX) & (NX - 1)
    dc = ((device & 1) - core + NC) & (NC - 1)
    term = lax.broadcasted_iota(jnp.int32, (8, B), 0)
    block = lax.broadcasted_iota(jnp.int32, (8, B), 1)
    real = block < BLOCKS
    offset = jnp.where(real, (dz * NX + dx) * NC + dc, PEERS).astype(f32)
    tag = (local * 8 + term).astype(f32)
    number = (block * 8 + term).astype(f32)
    fill = jnp.zeros((B - 8, B), f32)
    offset_t = jnp.concatenate([offset, fill], axis=0).T[:BLOCKS]
    number_t = jnp.concatenate([number, fill], axis=0).T[:BLOCKS]
    lanes = lax.broadcasted_iota(jnp.int32, (BLOCKS, 2 * B), 1).astype(f32)
    into = lax.broadcasted_iota(jnp.int32, (PEERS, B), 0).astype(f32)
    lane = lax.broadcasted_iota(jnp.int32, (PEERS, B), 1)
    source_col = lax.broadcasted_iota(jnp.int32, (BLOCKS, 1), 0).astype(f32)
    item = jnp.zeros((1, 2 * B), f32)
    source = jnp.zeros((1, 2 * B), f32)
    tags = jnp.full((PEERS, B), float(BLOCKS * 8), f32)
    for w in range(TERMS):
        rank_col = jnp.zeros((BLOCKS, 1), f32)
        rank_row = jnp.zeros((1, B), f32)
        for other in range(TERMS):
            met = (offset_t[:, w : w + 1] == offset[other : other + 1]) & (
                number[other : other + 1] < number_t[:, w : w + 1]
            )
            rank_col += jnp.sum(jnp.where(met, 1.0, 0.0), axis=1, keepdims=True)
            met = (offset_t[:, other : other + 1] == offset[w : w + 1]) & (
                number_t[:, other : other + 1] < number[w : w + 1]
            )
            rank_row += jnp.sum(jnp.where(met, 1.0, 0.0), axis=0, keepdims=True)
        slot = offset_t[:, w : w + 1] * CAP + rank_col
        at = jnp.where(lanes == slot, 1.0, 0.0)
        item += jnp.sum(at * (source_col + w * BLOCKS), axis=0, keepdims=True)
        source += jnp.sum(at * source_col, axis=0, keepdims=True)
        for k in range(CAP):
            met = (offset[w : w + 1] == into) & (rank_row == k)
            value = jnp.sum(jnp.where(met, tag[w : w + 1] + 1.0, 0.0), axis=1, keepdims=True)
            tags = jnp.where((lane == k) & (value > 0.0), value - 1.0, tags)
    return item.astype(jnp.int32), source.astype(jnp.int32), tags.astype(jnp.int32)


def main_kernel(
    energy, target_ref, v_ref, right_hbm, left_hbm, out_ref,
    tag_ref, slot_v, slot,
    right, left, right_t, going, arrived, segment, tags_in, table_v, table,
    rs_going, rs_arrived, own, v_t, second_t, out_t, ss_mine, ss_y, ss_x, ss_z,
    load_sem, tag_send, tag_recv, table_sem, go_send, go_recv, self_sem,
    rs_send, rs_recv, ag_send, ag_recv, ss_send, ss_recv,
):
    here = coordinates()
    z, x, core, y = here
    sec = (z * NX + x) * NC + core

    def y_peer(d):
        return (sec, (y + d) % NY)

    barrier = pltpu.get_barrier_semaphore()

    def greet(o, _):
        pl.semaphore_signal(barrier, inc=1, device_id=peer_of(o, here), device_id_type=MESH)
        return 0

    load_right = pltpu.make_async_copy(right_hbm, right, load_sem.at[0])
    load_left = pltpu.make_async_copy(left_hbm, left, load_sem.at[1])
    load_right.start()
    load_left.start()
    lax.fori_loop(1, PEERS, greet, 0)
    for d in range(1, NY):
        pl.semaphore_signal(barrier, inc=1, device_id=y_peer(d), device_id_type=MESH)
    item_row, source_row, tags = slot_tables(target_ref[...], here)
    slot_v[...] = jnp.concatenate([item_row, source_row, jnp.zeros((6, 2 * B), jnp.int32)], axis=0)
    to_scalar = pltpu.make_async_copy(slot_v, slot, table_sem)
    to_scalar.start()
    tag_ref[...] = jnp.broadcast_to(tags[:, None, :], (PEERS, 8, B))
    to_scalar.wait()
    load_right.wait()

    def remote(src, dst, send, recv, device):
        return pltpu.make_async_remote_copy(
            src_ref=src, dst_ref=dst, send_sem=send, recv_sem=recv, device_id=device, device_id_type=MESH
        )

    def products(o, m):
        for k in range(CAP):
            q = o * CAP + k
            if m == 0:
                block = right[jnp.clip(slot[0, q], 0, ITEMS - 1)].T
                right_t[q] = block
                product = lax.dot_general(block, v_ref[jnp.clip(slot[1, q], 0, BLOCKS - 1)], NT, preferred_element_type=jnp.float32)
            else:
                product = lax.dot_general(
                    right_t[q], second_t[jnp.clip(slot[1, q], 0, BLOCKS - 1)], NN, preferred_element_type=jnp.float32
                )
            product = product.astype(jnp.bfloat16)
            for c in range(CHUNKS):
                going[c, q] = product[c * ROWS : (c + 1) * ROWS]

    def send(o, m, c):
        slots = pl.ds(o * CAP, CAP)
        remote(
            going.at[c, slots], arrived[m * CHUNKS + c].at[slots],
            go_send.at[m, c], go_recv.at[m, c], peer_of(o, here),
        ).start()

    def send_tag(o):
        remote(tag_ref.at[o], tags_in.at[o], tag_send, tag_recv, peer_of(o, here)).start()

    def keep_own(m, c):
        pltpu.make_async_copy(
            going.at[c, pl.ds(0, CAP)], arrived[m * CHUNKS + c].at[pl.ds(0, CAP)], self_sem.at[m, c]
        ).start()

    def wait_own(m, c):
        pltpu.make_async_copy(
            going.at[c, pl.ds(0, CAP)], arrived[m * CHUNKS + c].at[pl.ds(0, CAP)], self_sem.at[m, c]
        ).wait()

    others = pl.ds(CAP, SLOTS - CAP)

    def wait_arrived(m, c):
        wait_own(m, c)
        into = arrived[m * CHUNKS + c].at[others]
        pltpu.make_async_copy(into, into, go_recv.at[m, c]).wait()

    def wait_sent(m, c):
        out_of = going.at[c, others]
        pltpu.make_async_copy(out_of, out_of, go_send.at[m, c]).wait()

    def send_all(m, c):
        def one(i, _):
            send(offset_at(i), m, c)
            return 0

        lax.fori_loop(0, PEERS - 1, one, 0)
        keep_own(m, c)

    early = 8

    def compute_first(i, _):
        products(offset_at(i), 0)
        return 0

    def send_first(i, _):
        send(offset_at(i), 0, 0)
        send_tag(offset_at(i))
        return 0

    def both_first(i, _):
        compute_first(i, 0)
        send_first(i, 0)
        return 0

    lax.fori_loop(0, early, compute_first, 0)
    pl.semaphore_wait(barrier, PEERS - 1 + NY - 1)
    lax.fori_loop(0, early, send_first, 0)
    lax.fori_loop(early, PEERS - 1, both_first, 0)
    products(0, 0)
    tags_in[0] = tag_ref[0]
    keep_own(0, 0)
    for c in range(1, CHUNKS):
        send_all(0, c)

    for j in range(QUARTER):
        v_t[j] = v_ref[y * QUARTER + j].astype(jnp.float32).T

    out_of = tag_ref.at[pl.ds(1, PEERS - 1)]
    into = tags_in.at[pl.ds(1, PEERS - 1)]
    pltpu.make_async_copy(into, into, tag_recv).wait()
    tag_all = jnp.max(tags_in[...], axis=1)
    order = lax.broadcasted_iota(jnp.int32, (PEERS, B), 0) * CAP + lax.broadcasted_iota(jnp.int32, (PEERS, B), 1)
    key = (tag_all * 256 + order).astype(jnp.float32)
    blank = jnp.full((B - PEERS, B), 1e9, jnp.float32)
    key_rows = jnp.concatenate([key, blank], axis=0).T
    tag_f = tag_all.astype(jnp.float32)
    block_f = (tag_all // 8).astype(jnp.float32)
    block_rows = jnp.concatenate([block_f, blank], axis=0).T
    lanes = lax.broadcasted_iota(jnp.int32, (PEERS, 2 * B), 1).astype(jnp.float32)
    order_f = order.astype(jnp.float32)
    perm = jnp.zeros((1, 2 * B), jnp.float32)
    tag_sorted = jnp.zeros((1, 2 * B), jnp.float32)
    follows = jnp.zeros((1, 2 * B), jnp.float32)
    last = jnp.zeros((1, 2 * B), jnp.float32)
    present = jnp.zeros((1, 2 * B), jnp.float32)
    for k in range(CAP):
        key_col = key[:, k : k + 1]
        block_col = block_f[:, k : k + 1]
        position = jnp.zeros((PEERS, 1), jnp.float32)
        before = jnp.zeros((PEERS, 1), jnp.float32)
        for other in range(CAP):
            less = key_rows[other : other + 1] < key_col
            same = block_rows[other : other + 1] == block_col
            position += jnp.sum(jnp.where(less, 1.0, 0.0), axis=1, keepdims=True)
            before += jnp.sum(jnp.where(less & same, 1.0, 0.0), axis=1, keepdims=True)
        here_p = jnp.where(lanes == position, 1.0, 0.0)
        perm += jnp.sum(here_p * order_f[:, k : k + 1], axis=0, keepdims=True)
        tag_sorted += jnp.sum(here_p * tag_f[:, k : k + 1], axis=0, keepdims=True)
        follows += jnp.sum(here_p * jnp.where(before > 0.0, 1.0, 0.0), axis=0, keepdims=True)
        last += jnp.sum(jnp.where(block_col <= lanes, 1.0, 0.0), axis=0, keepdims=True)
        present += jnp.sum(jnp.where(block_col == lanes, 1.0, 0.0), axis=0, keepdims=True)
    tag_i = tag_sorted.astype(jnp.int32)
    left_i = tag_i % 8 * BLOCKS + tag_i // 8
    rows = [
        perm.astype(jnp.int32),
        left_i,
        follows.astype(jnp.int32),
        jnp.maximum(last.astype(jnp.int32) - 1, 0),
        jnp.minimum(present.astype(jnp.int32), 1),
        jnp.zeros((3, 2 * B), jnp.int32),
    ]
    table_v[...] = jnp.concatenate(rows, axis=0)
    to_scalar = pltpu.make_async_copy(table_v, table, table_sem)
    to_scalar.start()
    to_scalar.wait()
    load_left.wait()

    def left_products(m, c):
        blocks = arrived[m * CHUNKS + c]

        def step(p, total):
            product = lax.dot_general(
                blocks[jnp.clip(table[0, p], 0, SLOTS - 1)], left[jnp.clip(table[1, p], 0, ITEMS - 1)], NT, preferred_element_type=jnp.float32
            )
            total = jnp.where(table[2, p] > 0, total, 0.0) + product
            segment[p] = total
            return total

        lax.fori_loop(0, SLOTS, step, jnp.zeros((ROWS, B), jnp.float32), unroll=8)

        def finish(t, _):
            value = jnp.where(table[4, t] > 0, segment[jnp.clip(table[3, t], 0, SLOTS - 1)], 0.0)
            rs_going[m * CHUNKS + c, t] = value.astype(jnp.bfloat16)
            return 0

        lax.fori_loop(0, BLOCKS, finish, 0, unroll=4)

        def finish_own(j, _):
            t = y * QUARTER + j
            own[c, j] = jnp.where(table[4, t] > 0, segment[jnp.clip(table[3, t], 0, SLOTS - 1)], 0.0)
            return 0

        lax.fori_loop(0, QUARTER, finish_own, 0, unroll=4)

    def scatter_y(m, c, d):
        quarter = (y + d) % NY * QUARTER
        return remote(
            rs_going.at[m * CHUNKS + c, pl.ds(quarter, QUARTER)], rs_arrived.at[m * CHUNKS + c, d - 1],
            rs_send.at[m * CHUNKS + c, d - 1], rs_recv.at[m * CHUNKS + c, d - 1], y_peer(d),
        )

    def sum_y(m, c):
        total = own[c]
        for d in range(1, NY):
            scatter_y(m, c, d).wait_recv()
            total += rs_arrived[m * CHUNKS + c, d - 1].astype(jnp.float32)
        return total

    def gather_y(m, c, d):
        where = (second_t, out_t)[m].at[pl.ds(y * QUARTER, QUARTER), pl.ds(c * ROWS, ROWS)]
        return remote(where, where, ag_send.at[m * CHUNKS + c, d - 1], ag_recv.at[m * CHUNKS + c, d - 1], y_peer(d))

    def arrives_y(m, c, d):
        quarter = (y - d + NY) % NY * QUARTER
        where = (second_t, out_t)[m].at[pl.ds(quarter, QUARTER), pl.ds(c * ROWS, ROWS)]
        return remote(where, where, ag_send.at[m * CHUNKS + c, d - 1], ag_recv.at[m * CHUNKS + c, d - 1], y_peer(d))

    shift = energy[0]
    ss_mine[0] = jnp.zeros((8, B), jnp.float32)

    def correct(c):
        value = sum_y(0, c) - shift * v_t[:, c * ROWS : (c + 1) * ROWS, :]
        ss_mine[0] += jnp.sum((value * value).reshape(QUARTER * ROWS // 8, 8, B), axis=0)
        second_t[pl.ds(y * QUARTER, QUARTER), pl.ds(c * ROWS, ROWS)] = value.astype(jnp.bfloat16)
        for d in range(1, NY):
            gather_y(0, c, d).start()

    for c in range(CHUNKS):
        wait_arrived(0, c)
        left_products(0, c)
        for d in range(1, NY):
            scatter_y(0, c, d).start()
        if c > 0:
            correct(c - 1)
    correct(CHUNKS - 1)
    for c in range(CHUNKS):
        wait_sent(0, c)
        for d in range(1, NY):
            arrives_y(0, c, d).wait_recv()

    def both_second(i, _):
        products(offset_at(i), 1)
        send(offset_at(i), 1, 0)
        return 0

    lax.fori_loop(0, PEERS - 1, both_second, 0)
    products(0, 1)
    keep_own(1, 0)
    for c in range(1, CHUNKS):
        send_all(1, c)

    def exchange(stage, buffer, count, device):
        copies = [
            remote(ss_mine.at[stage], buffer.at[d - 1], ss_send.at[stage, d - 1], ss_recv.at[stage, d - 1], device(d))
            for d in range(1, count)
        ]
        for copy in copies:
            copy.start()
        total = ss_mine[stage]
        for d, copy in enumerate(copies):
            copy.wait()
            total += buffer[d]
        return total

    ss_mine[1] = exchange(0, ss_y, NY, y_peer)
    ss_mine[2] = exchange(1, ss_x, NX * NC, lambda d: peer_of(jnp.int32(d), here))
    squares = exchange(2, ss_z, NZ, lambda d: peer_of(jnp.int32(d * NX * NC), here))
    cells = PEERS * BLOCKS * B * B
    inverse = 1.0 / jnp.sqrt(jnp.sum(squares, keepdims=True) / cells + EPSILON)

    def result(c):
        value = sum_y(1, c) * inverse
        out_t[pl.ds(y * QUARTER, QUARTER), pl.ds(c * ROWS, ROWS)] = value.astype(jnp.bfloat16)
        for d in range(1, NY):
            gather_y(1, c, d).start()

    for c in range(CHUNKS):
        wait_arrived(1, c)
        left_products(1, c)
        for d in range(1, NY):
            scatter_y(1, c, d).start()
        if c > 0:
            result(c - 1)
    result(CHUNKS - 1)
    for c in range(CHUNKS):
        for d in range(1, NY):
            arrives_y(1, c, d).wait_recv()

    def turn(t, _):
        out_ref[t] = out_t[t].T
        return 0

    lax.fori_loop(0, BLOCKS, turn, 0, unroll=4)
    pltpu.make_async_copy(out_of, out_of, tag_send).wait()
    for c in range(CHUNKS):
        wait_sent(1, c)
        for m in range(2):
            for d in range(1, NY):
                scatter_y(m, c, d).wait_send()
                gather_y(m, c, d).wait_send()


def body(wavefunction, energy_shift, left_env, right_env, target):
    smem, vmem = pl.BlockSpec(memory_space=pltpu.SMEM), pl.BlockSpec(memory_space=pltpu.VMEM)
    hbm = pl.BlockSpec(memory_space=pl.ANY)
    bf16, f32 = jnp.bfloat16, jnp.float32
    dma, all_chunks = pltpu.SemaphoreType.DMA, 2 * CHUNKS
    scratch = [
        pltpu.VMEM((PEERS, 8, B), jnp.int32),
        pltpu.VMEM((8, 2 * B), jnp.int32),
        pltpu.SMEM((8, 2 * B), jnp.int32),
        pltpu.VMEM((ITEMS, B, B), bf16),
        pltpu.VMEM((ITEMS, B, B), bf16),
        pltpu.VMEM((SLOTS, B, B), bf16),
        pltpu.VMEM((CHUNKS, SLOTS, ROWS, B), bf16),
        [pltpu.VMEM((SLOTS, ROWS, B), bf16) for _ in range(all_chunks)],
        pltpu.VMEM((SLOTS, ROWS, B), f32),
        pltpu.VMEM((PEERS, 8, B), jnp.int32),
        pltpu.VMEM((8, 2 * B), jnp.int32),
        pltpu.SMEM((8, 2 * B), jnp.int32),
        pltpu.VMEM((all_chunks, BLOCKS, ROWS, B), bf16),
        pltpu.VMEM((all_chunks, NY - 1, QUARTER, ROWS, B), bf16),
        pltpu.VMEM((CHUNKS, QUARTER, ROWS, B), f32),
        pltpu.VMEM((QUARTER, B, B), f32),
        pltpu.VMEM((BLOCKS, B, B), bf16),
        pltpu.VMEM((BLOCKS, B, B), bf16),
        pltpu.VMEM((3, 8, B), f32),
        pltpu.VMEM((NY - 1, 8, B), f32),
        pltpu.VMEM((NX * NC - 1, 8, B), f32),
        pltpu.VMEM((NZ - 1, 8, B), f32),
        dma((2,)),
        dma,
        dma,
        dma,
        dma((2, CHUNKS)),
        dma((2, CHUNKS)),
        dma((2, CHUNKS)),
        dma((all_chunks, NY - 1)),
        dma((all_chunks, NY - 1)),
        dma((all_chunks, NY - 1)),
        dma((all_chunks, NY - 1)),
        dma((3, NZ - 1)),
        dma((3, NZ - 1)),
    ]
    return pl.pallas_call(
        main_kernel,
        out_shape=jax.ShapeDtypeStruct((BLOCKS, B, B), bf16),
        in_specs=[smem, vmem, vmem, hbm, hbm],
        out_specs=vmem,
        scratch_shapes=scratch,
        compiler_params=pltpu.CompilerParams(
            collective_id=0, has_side_effects=True, vmem_limit_bytes=58 * 2**20
        ),
        name="davidson",
    )(
        energy_shift, target, wavefunction,
        right_env.reshape(ITEMS, B, B), left_env.reshape(ITEMS, B, B),
    )


def solution(mesh):
    placed = (
        P("sec", None, None),
        P(),
        P("mpo", "sec", None, None),
        P("mpo", "sec", None, None),
        P("mpo", "sec"),
    )
    return jax.shard_map(
        body, mesh=mesh, in_specs=placed, out_specs=P("sec", None, None), check_vma=False
    )
```

time: 648 us -> 352 us (0.54)
  Pallas kernels: 0 us -> 349 us
  blocking collectives: 317 us -> 0 us
  waiting for transfers between devices: 199 us -> 0 us
  local copies, waits for them, and re-layouts: 51.6 us -> 2.31 us
  matrix products: 28.5 us -> 0 us
  starting transfers between devices: 22.8 us -> 0 us
  between operations: 14.9 us -> 0.66 us
  other arithmetic: 13.2 us -> 0 us
    pallas_call x0 -> x1, Pallas kernels: none -> 349 us  [body(): pl.pallas_call(main_kernel, out_shape=jax.ShapeDtypeStruct((BLOCKS, B, B)...]
    psum x2 -> x0, blocking collectives: 160 us -> none  [the longest x1 120 us: body(): corr_squares = lax.psum(jnp.sum(correction * correction), 'sec')]
    all_to_all x1 -> x0, blocking collectives: 156 us -> none  [partial_image(): lax.all_to_all(outgoing, 'sec', split_axis=0, concat_axis=0, tiled=True)]
    all_to_all x2 -> x0, waiting for transfers between devices: 140 us -> none  [the longest x1 140 us: partial_image(): lax.all_to_all(outgoing, 'sec', split_axis=0, concat_axis=0, tiled=True)]
    psum x1 -> x0, waiting for transfers between devices: 59.3 us -> none  [combine_whole(): return lax.psum(partial_terms, 'mpo')]
    dot_general x6 -> x0, matrix products: 28.5 us -> none  [the longest x2 11.9 us: partial_image(): jnp.dot(selector, arrived.reshape(arrived.shape[0], row_size * col_size),...]
    all_to_all x2 -> x0, starting transfers between devices: 22.6 us -> none  [the longest x1 12 us: partial_image(): lax.all_to_all(slot_tag, 'sec', split_axis=0, concat_axis=0, tiled=True)]
    gather x2 -> x0, local copies, waits for them, and re-layouts: 21.1 us -> none  [partial_image(): outgoing = jnp.take(padded, slot_item, axis=0)]
  transfers between devices with their start and end apart: 3 -> 0, of which waited for: 2 -> 0; matrix products, arithmetic and copies ran while one was open for 6% -> 0% of each run, Pallas kernels for 0% -> 0%
where the time goes in v1:
time: 352 us
  Pallas kernels  349 us (99%)
    pallas_call x1, Pallas kernels, body(): pl.pallas_call(main_kernel, out_shape=jax.ShapeDtypeStruct((BLOCKS, B, B)...  349 us

profile of v1, /device:TPU:4, one launch (start us, length us, event | category | flops | bytes accessed | tf_op | source)
XLA Modules:
  0.0 351.6 jit_solution(1384898722664586900)
XLA Ops:
  0.7 348.6 %davidson.1 = bf16[32,128,128]{2,1,0:T(8,128)(2,1)} custom-call(f32[1]{0:T(128)S(6)} %copy.7.energy, s32[5,32]{1,0:T(8,128)} %target_ref.1, bf16[32,128,128]{2,1,0:T(8,128)(2,1)} %v_ref.1, bf16[160,128,128]{2,1,0:T(8,128)(2,1)} %bitcast.2, bf16[160,128,128]{2,1,0:T(8,128)(2,1)} %bitcast.3), custom_call_target="tpu_custom_call" | custom-call | tf_op jit(solution)/shard_map/davidson/pallas_call | solution.py:443
  349.3 2.3 copy.8

commit v2 on v1

--- a/solution.py
+++ b/solution.py
@@ -17,8 +17,9 @@
 BLOCKS = 32
 TERMS = 5
 ITEMS = TERMS * BLOCKS
-CHUNKS = 4
-ROWS = B // CHUNKS
+ROWS = (48, 48, 16, 16)
+START = tuple(sum(ROWS[:c]) for c in range(len(ROWS)))
+CHUNKS = len(ROWS)
 QUARTER = BLOCKS // NY
 NT = (((1,), (1,)), ((), ()))
 NN = (((1,), (0,)), ((), ()))
@@ -93,7 +94,7 @@
     energy, target_ref, v_ref, right_hbm, left_hbm, out_ref,
     tag_ref, slot_v, slot,
     right, left, right_t, going, arrived, segment, tags_in, table_v, table,
-    rs_going, rs_arrived, own, v_t, second_t, out_t, ss_mine, ss_y, ss_x, ss_z,
+    rs_going, rs_arrived, own, v_t, second_t, ss_mine, ss_y, ss_x, ss_z,
     load_sem, tag_send, tag_recv, table_sem, go_send, go_recv, self_sem,
     rs_send, rs_recv, ag_send, ag_recv, ss_send, ss_recv,
 ):
@@ -143,12 +144,12 @@
                 )
             product = product.astype(jnp.bfloat16)
             for c in range(CHUNKS):
-                going[c, q] = product[c * ROWS : (c + 1) * ROWS]
+                going[c][q] = product[START[c] : START[c] + ROWS[c]]
 
     def send(o, m, c):
         slots = pl.ds(o * CAP, CAP)
         remote(
-            going.at[c, slots], arrived[m * CHUNKS + c].at[slots],
+            going[c].at[slots], arrived[m * CHUNKS + c].at[slots],
             go_send.at[m, c], go_recv.at[m, c], peer_of(o, here),
         ).start()
 
@@ -157,12 +158,12 @@
 
     def keep_own(m, c):
         pltpu.make_async_copy(
-            going.at[c, pl.ds(0, CAP)], arrived[m * CHUNKS + c].at[pl.ds(0, CAP)], self_sem.at[m, c]
+            going[c].at[pl.ds(0, CAP)], arrived[m * CHUNKS + c].at[pl.ds(0, CAP)], self_sem.at[m, c]
         ).start()
 
     def wait_own(m, c):
         pltpu.make_async_copy(
-            going.at[c, pl.ds(0, CAP)], arrived[m * CHUNKS + c].at[pl.ds(0, CAP)], self_sem.at[m, c]
+            going[c].at[pl.ds(0, CAP)], arrived[m * CHUNKS + c].at[pl.ds(0, CAP)], self_sem.at[m, c]
         ).wait()
 
     others = pl.ds(CAP, SLOTS - CAP)
@@ -173,7 +174,7 @@
         pltpu.make_async_copy(into, into, go_recv.at[m, c]).wait()
 
     def wait_sent(m, c):
-        out_of = going.at[c, others]
+        out_of = going[c].at[others]
         pltpu.make_async_copy(out_of, out_of, go_send.at[m, c]).wait()
 
     def send_all(m, c):
@@ -184,7 +185,7 @@
         lax.fori_loop(0, PEERS - 1, one, 0)
         keep_own(m, c)
 
-    early = 8
+    early = 16
 
     def compute_first(i, _):
         products(offset_at(i), 0)
@@ -207,8 +208,7 @@
     products(0, 0)
     tags_in[0] = tag_ref[0]
     keep_own(0, 0)
-    for c in range(1, CHUNKS):
-        send_all(0, c)
+    send_all(0, 1)
 
     for j in range(QUARTER):
         v_t[j] = v_ref[y * QUARTER + j].astype(jnp.float32).T
@@ -263,29 +263,36 @@
     to_scalar.wait()
     load_left.wait()
 
+    def turn_left(n, _):
+        left[n] = left[n].T
+        return 0
+
+    lax.fori_loop(0, ITEMS, turn_left, 0, unroll=4)
+
     def left_products(m, c):
         blocks = arrived[m * CHUNKS + c]
 
         def step(p, total):
             product = lax.dot_general(
-                blocks[jnp.clip(table[0, p], 0, SLOTS - 1)], left[jnp.clip(table[1, p], 0, ITEMS - 1)], NT, preferred_element_type=jnp.float32
+                blocks[jnp.clip(table[0, p], 0, SLOTS - 1)], left[jnp.clip(table[1, p], 0, ITEMS - 1)], NN, preferred_element_type=jnp.float32
             )
             total = jnp.where(table[2, p] > 0, total, 0.0) + product
-            segment[p] = total
+            segment[p, : ROWS[c]] = total
             return total
 
-        lax.fori_loop(0, SLOTS, step, jnp.zeros((ROWS, B), jnp.float32), unroll=8)
+        lax.fori_loop(0, SLOTS, step, jnp.zeros((ROWS[c], B), jnp.float32), unroll=8)
 
         def finish(t, _):
-            value = jnp.where(table[4, t] > 0, segment[jnp.clip(table[3, t], 0, SLOTS - 1)], 0.0)
-            rs_going[m * CHUNKS + c, t] = value.astype(jnp.bfloat16)
+            value = jnp.where(table[4, t] > 0, segment[jnp.clip(table[3, t], 0, SLOTS - 1), : ROWS[c]], 0.0)
+            rs_going[m * CHUNKS + c][t] = value.astype(jnp.bfloat16)
             return 0
 
         lax.fori_loop(0, BLOCKS, finish, 0, unroll=4)
 
+    def own_quarter(c):
         def finish_own(j, _):
             t = y * QUARTER + j
-            own[c, j] = jnp.where(table[4, t] > 0, segment[jnp.clip(table[3, t], 0, SLOTS - 1)], 0.0)
+            own[c][j] = jnp.where(table[4, t] > 0, segment[jnp.clip(table[3, t], 0, SLOTS - 1), : ROWS[c]], 0.0)
             return 0
 
         lax.fori_loop(0, QUARTER, finish_own, 0, unroll=4)
@@ -293,102 +300,117 @@
     def scatter_y(m, c, d):
         quarter = (y + d) % NY * QUARTER
         return remote(
-            rs_going.at[m * CHUNKS + c, pl.ds(quarter, QUARTER)], rs_arrived.at[m * CHUNKS + c, d - 1],
+            rs_going[m * CHUNKS + c].at[pl.ds(quarter, QUARTER)], rs_arrived[m * CHUNKS + c].at[d - 1],
             rs_send.at[m * CHUNKS + c, d - 1], rs_recv.at[m * CHUNKS + c, d - 1], y_peer(d),
         )
 
     def sum_y(m, c):
-        total = own[c]
+        total = own[c][...]
         for d in range(1, NY):
             scatter_y(m, c, d).wait_recv()
-            total += rs_arrived[m * CHUNKS + c, d - 1].astype(jnp.float32)
+            total += rs_arrived[m * CHUNKS + c][d - 1].astype(jnp.float32)
         return total
 
     def gather_y(m, c, d):
-        where = (second_t, out_t)[m].at[pl.ds(y * QUARTER, QUARTER), pl.ds(c * ROWS, ROWS)]
+        where = (second_t, out_ref)[m].at[pl.ds(y * QUARTER, QUARTER), pl.ds(START[c], ROWS[c])]
         return remote(where, where, ag_send.at[m * CHUNKS + c, d - 1], ag_recv.at[m * CHUNKS + c, d - 1], y_peer(d))
 
     def arrives_y(m, c, d):
         quarter = (y - d + NY) % NY * QUARTER
-        where = (second_t, out_t)[m].at[pl.ds(quarter, QUARTER), pl.ds(c * ROWS, ROWS)]
+        where = (second_t, out_ref)[m].at[pl.ds(quarter, QUARTER), pl.ds(START[c], ROWS[c])]
         return remote(where, where, ag_send.at[m * CHUNKS + c, d - 1], ag_recv.at[m * CHUNKS + c, d - 1], y_peer(d))
 
     shift = energy[0]
     ss_mine[0] = jnp.zeros((8, B), jnp.float32)
 
     def correct(c):
-        value = sum_y(0, c) - shift * v_t[:, c * ROWS : (c + 1) * ROWS, :]
-        ss_mine[0] += jnp.sum((value * value).reshape(QUARTER * ROWS // 8, 8, B), axis=0)
-        second_t[pl.ds(y * QUARTER, QUARTER), pl.ds(c * ROWS, ROWS)] = value.astype(jnp.bfloat16)
+        value = sum_y(0, c) - shift * v_t[:, START[c] : START[c] + ROWS[c], :]
+        ss_mine[0] += jnp.sum((value * value).reshape(QUARTER * ROWS[c] // 8, 8, B), axis=0)
+        second_t[pl.ds(y * QUARTER, QUARTER), pl.ds(START[c], ROWS[c])] = value.astype(jnp.bfloat16)
         for d in range(1, NY):
             gather_y(0, c, d).start()
 
-    for c in range(CHUNKS):
-        wait_arrived(0, c)
-        left_products(0, c)
-        for d in range(1, NY):
-            scatter_y(0, c, d).start()
-        if c > 0:
-            correct(c - 1)
-    correct(CHUNKS - 1)
-    for c in range(CHUNKS):
-        wait_sent(0, c)
-        for d in range(1, NY):
-            arrives_y(0, c, d).wait_recv()
-
-    def both_second(i, _):
-        products(offset_at(i), 1)
-        send(offset_at(i), 1, 0)
-        return 0
-
-    lax.fori_loop(0, PEERS - 1, both_second, 0)
-    products(0, 1)
-    keep_own(1, 0)
-    for c in range(1, CHUNKS):
-        send_all(1, c)
-
-    def exchange(stage, buffer, count, device):
-        copies = [
+    def exchange(stage):
+        buffer, count, device = (
+            (ss_y, NY, y_peer),
+            (ss_x, NX * NC, lambda d: peer_of(jnp.int32(d), here)),
+            (ss_z, NZ, lambda d: peer_of(jnp.int32(d * NX * NC), here)),
+        )[stage]
+        return buffer, [
             remote(ss_mine.at[stage], buffer.at[d - 1], ss_send.at[stage, d - 1], ss_recv.at[stage, d - 1], device(d))
             for d in range(1, count)
         ]
-        for copy in copies:
+
+    def start_exchange(stage):
+        for copy in exchange(stage)[1]:
             copy.start()
+
+    def finish_exchange(stage):
+        buffer, copies = exchange(stage)
         total = ss_mine[stage]
         for d, copy in enumerate(copies):
             copy.wait()
             total += buffer[d]
         return total
 
-    ss_mine[1] = exchange(0, ss_y, NY, y_peer)
-    ss_mine[2] = exchange(1, ss_x, NX * NC, lambda d: peer_of(jnp.int32(d), here))
-    squares = exchange(2, ss_z, NZ, lambda d: peer_of(jnp.int32(d * NX * NC), here))
-    cells = PEERS * BLOCKS * B * B
-    inverse = 1.0 / jnp.sqrt(jnp.sum(squares, keepdims=True) / cells + EPSILON)
-
-    def result(c):
+    for c in range(CHUNKS):
+        wait_arrived(0, c)
+        left_products(0, c)
+        for d in range(1, NY):
+            scatter_y(0, c, d).start()
+        own_quarter(c)
+        if c + 2 < CHUNKS:
+            send_all(0, c + 2)
+        if c > 0:
+            correct(c - 1)
+    correct(CHUNKS - 1)
+    start_exchange(0)
+    for c in range(CHUNKS):
+        wait_sent(0, c)
+        for d in range(1, NY):
+            arrives_y(0, c, d).wait_recv()
+
+    ss_mine[1] = finish_exchange(0)
+    start_exchange(1)
+
+    def both_second(i, _):
+        products(offset_at(i), 1)
+        send(offset_at(i), 1, 0)
+        return 0
+
+    lax.fori_loop(0, PEERS - 1, both_second, 0)
+    products(0, 1)
+    keep_own(1, 0)
+    ss_mine[2] = finish_exchange(1)
+    start_exchange(2)
+    send_all(1, 1)
+
+    def result(c, inverse):
         value = sum_y(1, c) * inverse
-        out_t[pl.ds(y * QUARTER, QUARTER), pl.ds(c * ROWS, ROWS)] = value.astype(jnp.bfloat16)
+        out_ref[pl.ds(y * QUARTER, QUARTER), pl.ds(START[c], ROWS[c])] = value.astype(jnp.bfloat16)
         for d in range(1, NY):
             gather_y(1, c, d).start()
 
+    inverse = None
     for c in range(CHUNKS):
         wait_arrived(1, c)
         left_products(1, c)
         for d in range(1, NY):
             scatter_y(1, c, d).start()
-        if c > 0:
-            result(c - 1)
-    result(CHUNKS - 1)
+        own_quarter(c)
+        if c + 2 < CHUNKS:
+            send_all(1, c + 2)
+        if c == 0:
+            squares = finish_exchange(2)
+            cells = PEERS * BLOCKS * B * B
+            inverse = 1.0 / jnp.sqrt(jnp.sum(squares, keepdims=True) / cells + EPSILON)
+        else:
+            result(c - 1, inverse)
+    result(CHUNKS - 1, inverse)
     for c in range(CHUNKS):
         for d in range(1, NY):
             arrives_y(1, c, d).wait_recv()
 
-    def turn(t, _):
-        out_ref[t] = out_t[t].T
-        return 0
-
-    lax.fori_loop(0, BLOCKS, turn, 0, unroll=4)
     pltpu.make_async_copy(out_of, out_of, tag_send).wait()
     for c in range(CHUNKS):
         wait_sent(1, c)
@@ -410,17 +432,16 @@
         pltpu.VMEM((ITEMS, B, B), bf16),
         pltpu.VMEM((ITEMS, B, B), bf16),
         pltpu.VMEM((SLOTS, B, B), bf16),
-        pltpu.VMEM((CHUNKS, SLOTS, ROWS, B), bf16),
-        [pltpu.VMEM((SLOTS, ROWS, B), bf16) for _ in range(all_chunks)],
-        pltpu.VMEM((SLOTS, ROWS, B), f32),
+        [pltpu.VMEM((SLOTS, rows, B), bf16) for rows in ROWS],
+        [pltpu.VMEM((SLOTS, rows, B), bf16) for rows in 2 * ROWS],
+        pltpu.VMEM((SLOTS, max(ROWS), B), f32),
         pltpu.VMEM((PEERS, 8, B), jnp.int32),
         pltpu.VMEM((8, 2 * B), jnp.int32),
         pltpu.SMEM((8, 2 * B), jnp.int32),
-        pltpu.VMEM((all_chunks, BLOCKS, ROWS, B), bf16),
-        pltpu.VMEM((all_chunks, NY - 1, QUARTER, ROWS, B), bf16),
-        pltpu.VMEM((CHUNKS, QUARTER, ROWS, B), f32),
+        [pltpu.VMEM((BLOCKS, rows, B), bf16) for rows in 2 * ROWS],
+        [pltpu.VMEM((NY - 1, QUARTER, rows, B), bf16) for rows in 2 * ROWS],
+        [pltpu.VMEM((QUARTER, rows, B), f32) for rows in ROWS],
         pltpu.VMEM((QUARTER, B, B), f32),
-        pltpu.VMEM((BLOCKS, B, B), bf16),
         pltpu.VMEM((BLOCKS, B, B), bf16),
         pltpu.VMEM((3, 8, B), f32),
         pltpu.VMEM((NY - 1, 8, B), f32),
@@ -440,7 +461,7 @@
         dma((3, NZ - 1)),
         dma((3, NZ - 1)),
     ]
-    return pl.pallas_call(
+    transposed = pl.pallas_call(
         main_kernel,
         out_shape=jax.ShapeDtypeStruct((BLOCKS, B, B), bf16),
         in_specs=[smem, vmem, vmem, hbm, hbm],
@@ -454,6 +475,7 @@
         energy_shift, target, wavefunction,
         right_env.reshape(ITEMS, B, B), left_env.reshape(ITEMS, B, B),
     )
+    return jnp.swapaxes(transposed, 1, 2)
 
 
 def solution(mesh):

time: 352 us -> 325 us (0.923)
  Pallas kernels: 349 us -> 321 us
    pallas_call x1, Pallas kernels: 349 us -> 321 us  [body(): pl.pallas_call(main_kernel, out_shape=jax.ShapeDtypeStruct((BLOCKS, B, B)...]
where the time goes in v2:
time: 325 us; the launch traced here: 324 us
  Pallas kernels  321 us (99%)
    pallas_call x1, Pallas kernels, body(): pl.pallas_call(main_kernel, out_shape=jax.ShapeDtypeStruct((BLOCKS, B, B)...  321 us

profile of v2, /device:TPU:4, one launch (start us, length us, event | category | flops | bytes accessed | tf_op | source)
XLA Modules:
  0.0 324.2 jit_solution(3837322277052493599)
XLA Ops:
  0.7 321.3 %davidson.1 = bf16[32,128,128]{2,1,0:T(8,128)(2,1)} custom-call(f32[1]{0:T(128)S(6)} %copy.7.energy, s32[5,32]{1,0:T(8,128)} %target_ref.1, bf16[32,128,128]{2,1,0:T(8,128)(2,1)} %v_ref.1, bf16[160,128,128]{2,1,0:T(8,128)(2,1)} %bitcast.3, bf16[160,128,128]{2,1,0:T(8,128)(2,1)} %bitcast.4), custom_call_target="tpu_custom_call" | custom-call | tf_op jit(solution)/shard_map/davidson/pallas_call | solution.py:464
  322.0 2.3 copy.6
